TPU v7x, 32 devices: a whole 2x2x4 slice. The times are simulated.
32 devices in a mesh: gx: 4 (over y, core), gy: 8 (over z, x).
Axes of the slice: x: 2, y: 2, z: 4, core: 2. Of those that a mesh axis runs over, the one named last changes fastest.
Arguments:
- rhs: float32 [32, 64, 512], P('gx', 'gy'), may hold values from -18 to 18
- diag: float32 [32, 64, 512], P('gx', 'gy'), may hold values from 0.5 to 2
- smoother_center: float32 [32, 64, 512], P('gx', 'gy'), may hold values from 0.1 to 0.2
- smoother_faces: float32 [6, 32, 64, 512], P(None, 'gx', 'gy'), may hold values from 0.01 to 0.05
- send_count: int32 [4, 8, 8], P('gx', 'gy'), may hold values from 0 to 4096, as said below
- send_cell: int32 [4, 8, 8, 4096], P('gx', 'gy'), may hold values from 0 to 32767, as said below
- restrict_col: int32 [27, 4, 8, 4096], P(None, 'gx', 'gy'), may hold values from 0 to 65535, as said below
- restrict_vals: float32 [27, 4, 8, 4096], P(None, 'gx', 'gy'), may hold values from 0.03 to 0.2
- coarse_col: int32 [16, 4, 8, 4096], P(None, 'gx', 'gy'), may hold values from 0 to 12287, as said below
- coarse_diag: float32 [4, 8, 4096], P('gx', 'gy'), may hold values from 3 to 6
- coarse_vals: float32 [16, 4, 8, 4096], P(None, 'gx', 'gy'), may hold values from -3 to 3
- csmooth_diag: float32 [4, 8, 4096], P('gx', 'gy'), may hold values from 0.15 to 0.3
- csmooth_vals: float32 [16, 4, 8, 4096], P(None, 'gx', 'gy'), may hold values from -0.3 to 0.3
- remote_row: int32 [4, 4, 8, 8, 4096], P(None, 'gx', 'gy'), may hold values from 0 to 4095, as said below
- remote_vals: float32 [4, 4, 8, 8, 4096], P(None, 'gx', 'gy'), may hold values from 0.3 to 1
- interp_row: int32 [4, 32, 64, 512], P(None, 'gx', 'gy'), may hold values from 0 to 4095, as said below
- interp_vals: float32 [4, 32, 64, 512], P(None, 'gx', 'gy'), may hold values from 0.3 to 1
Outputs:
- solution: float32 [32, 64, 512], P('gx', 'gy')
- residual: float32 [32, 64, 512], P('gx', 'gy')
Inputs may be any that keep to these rules, and one draw needn't show every extreme that they name: `send_count`: zero towards a neighbour outside the grid; one device receives 4096 used slots from each of its eight neighbours, and about a quarter of the devices receive several times more than the rest. `send_cell`: the cell of a slot towards direction d lies within 2 cells of the side facing that neighbour, within 4 cells of both sides for a diagonal neighbour. The slots of one direction in one aligned block of 128 slots lie in one run of 128 cells along z that starts at a multiple of 128. `restrict_col`: only a device's first 1024 coarse rows read received slots. For one k, the entries of one aligned block of 128 coarse rows lie in one aligned block of 128 columns. `coarse_col`: only a device's first 1024 coarse rows read neighbours' rows. For one k, the entries of one aligned block of 128 coarse rows lie in one aligned block of 128 columns. `remote_row`: for one k and one direction, the entries of one aligned block of 128 slots lie in one aligned block of 128 coarse rows. `interp_row`: for one k, the entries of one run of 128 cells along z that starts at a multiple of 128 lie in one aligned block of 128 coarse rows.
All inputs are finite; a program needn't handle non-finite values.
Results may differ from a plain program's by a relative error of at most 0.0003.
Values sent between devices are 32-bit elements; how exact they have to be, the bound alone decides.
A program may use at most 128 MiB of HBM per device.

v0:
```python
import jax
import jax.numpy as jnp
from jax import lax
from jax.sharding import PartitionSpec as P

BLK = 128
NRIM = 1024


def extended(array, sides, width):
    for axis, dim in sides:
        size, length = (lax.axis_size(axis), array.shape[dim])
        up = [(i, (i + 1) % size) for i in range(size - 1)]
        down = [(j, i) for i, j in up]
        last = lax.slice_in_dim(array, length - width, length, axis=dim)
        first = lax.slice_in_dim(array, 0, width, axis=dim)
        before = lax.ppermute(last, axis, up)
        after = lax.ppermute(first, axis, down)
        array = jnp.concatenate([before, array, after], axis=dim)
    return array


def stencil_parts(padded):
    wider = jnp.pad(padded, ((0, 0), (0, 0), (1, 1)))
    centre = wider[1:-1, 1:-1, 1:-1]
    beside = [
        wider[:-2, 1:-1, 1:-1],
        wider[2:, 1:-1, 1:-1],
        wider[1:-1, :-2, 1:-1],
        wider[1:-1, 2:, 1:-1],
        wider[1:-1, 1:-1, :-2],
        wider[1:-1, 1:-1, 2:],
    ]
    return (centre, beside)


def operator_from(padded, diag):
    centre, beside = stencil_parts(padded)
    beside_sum = beside[0]
    for which in range(1, 6):
        beside_sum = beside_sum + beside[which]
    return (6.0 + diag) * centre - beside_sum


def smoother_from(padded, center, faces):
    centre, beside = stencil_parts(padded)
    result = center * centre
    for which in range(6):
        result = result + faces[which] * beside[which]
    return result


def with_rim(field):
    return extended(field, (("gx", 0), ("gy", 1)), 1)


def block_select(column, table_blocks):
    grouped = column.reshape(column.shape[:-1] + (column.shape[-1] // BLK, BLK))
    base = grouped[..., 0] // BLK
    choose = base[..., None] == lax.broadcasted_iota(
        jnp.int32, base.shape + (table_blocks,), base.ndim
    )
    within = (grouped % BLK)[..., None] == lax.broadcasted_iota(
        jnp.int32, grouped.shape + (BLK,), grouped.ndim
    )
    return (choose.astype(jnp.float32), within)


def block_read(table, column):
    table_blocks = table.reshape(-1, BLK)
    choose, within = block_select(column, table_blocks.shape[0])
    rows = jnp.einsum("...t,tb->...b", choose, table_blocks, precision=lax.Precision.HIGHEST)
    picked = jnp.sum(jnp.where(within, rows[..., None, :], jnp.float32(0.0)), axis=-1)
    return picked.reshape(column.shape)


def block_add(values, column, length):
    choose, within = block_select(column, length // BLK)
    grouped = values.reshape(within.shape[:-1])
    spread = jnp.sum(jnp.where(within, grouped[..., None], jnp.float32(0.0)), axis=-2)
    total = jnp.einsum(
        "st,sb->tb",
        choose.reshape(-1, length // BLK),
        spread.reshape(-1, BLK),
        precision=lax.Precision.HIGHEST,
    )
    return total.reshape(-1)


def nine_blocks(per_side):
    blank = jnp.zeros((1, per_side.shape[-1]), per_side.dtype)
    return jnp.concatenate([per_side[:4], blank, per_side[4:]], axis=0).reshape(
        3, 3, per_side.shape[-1]
    )


def outer_eight(block_grid):
    flat_blocks = block_grid.reshape(9, block_grid.shape[-1])
    return jnp.concatenate([flat_blocks[:4], flat_blocks[5:]], axis=0)


def slots_to_owners(per_side):
    blocks = nine_blocks(per_side)
    padded = extended(blocks, (("gx", 0), ("gy", 1)), 1)
    return outer_eight(padded[0::2, 0::2])


def slots_to_senders(per_side):
    blocks = nine_blocks(per_side)
    padded = extended(blocks, (("gx", 0), ("gy", 1)), 1)
    return outer_eight(padded[0::2, 0::2])


def coarse_apply(vector, diagonal, values, column):
    padded = extended(vector[:, :, :NRIM], (("gx", 0), ("gy", 1)), 1)
    coarse_table = jnp.concatenate([vector.reshape(-1), outer_eight(padded).reshape(-1)])
    gathered = block_read(coarse_table, column)
    return diagonal * vector + jnp.sum(values * gathered, axis=0)


def body(
    rhs,
    diag,
    smoother_center,
    smoother_faces,
    send_count,
    send_cell,
    restrict_col,
    restrict_vals,
    coarse_col,
    coarse_diag,
    coarse_vals,
    csmooth_diag,
    csmooth_vals,
    remote_row,
    remote_vals,
    interp_row,
    interp_vals,
):
    x_first = smoother_from(with_rim(rhs), smoother_center, smoother_faces)
    r_first = rhs - operator_from(with_rim(x_first), diag)
    flat_first = r_first.reshape(-1)
    cell_ids = send_cell.reshape(8, -1)
    slot_ids = lax.broadcasted_iota(jnp.int32, cell_ids.shape, 1)
    is_live = slot_ids < send_count.reshape(8, 1)
    sent_vals = jnp.where(is_live, block_read(flat_first, cell_ids), jnp.float32(0.0))
    received = slots_to_owners(sent_vals)
    fine_table = jnp.concatenate([flat_first, received.reshape(-1)])
    coarse_rhs = jnp.sum(restrict_vals * block_read(fine_table, restrict_col), axis=0)
    coarse_first = coarse_apply(coarse_rhs, csmooth_diag, csmooth_vals, coarse_col)
    coarse_resid = coarse_rhs - coarse_apply(coarse_first, coarse_diag, coarse_vals, coarse_col)
    coarse_second = coarse_first + coarse_apply(
        coarse_resid, csmooth_diag, csmooth_vals, coarse_col
    )
    second_flat = coarse_second.reshape(-1)
    back_vals = jnp.sum(remote_vals * block_read(second_flat, remote_row), axis=0).reshape(8, -1)
    returned = jnp.where(is_live, slots_to_senders(back_vals), jnp.float32(0.0))
    local_part = jnp.sum(interp_vals * block_read(second_flat, interp_row), axis=0)
    scattered = block_add(returned, cell_ids, flat_first.shape[0])
    x_second = x_first + (local_part + scattered.reshape(rhs.shape))
    r_second = rhs - operator_from(with_rim(x_second), diag)
    solution = x_second + smoother_from(with_rim(r_second), smoother_center, smoother_faces)
    residual = rhs - operator_from(with_rim(solution), diag)
    return (solution, residual)


def solution(mesh):
    placed = (
        P("gx", "gy", None),
        P("gx", "gy", None),
        P("gx", "gy", None),
        P(None, "gx", "gy", None),
        P("gx", "gy", None),
        P("gx", "gy", None, None),
        P(None, "gx", "gy", None),
        P(None, "gx", "gy", None),
        P(None, "gx", "gy", None),
        P("gx", "gy", None),
        P(None, "gx", "gy", None),
        P("gx", "gy", None),
        P(None, "gx", "gy", None),
        P(None, "gx", "gy", None, None),
        P(None, "gx", "gy", None, None),
        P(None, "gx", "gy", None),
        P(None, "gx", "gy", None),
    )
    return jax.shard_map(
        body,
        mesh=mesh,
        in_specs=placed,
        out_specs=(P("gx", "gy", None), P("gx", "gy", None)),
        check_vma=False,
    )
```

profile of v0, /device:TPU:1, one launch (start us, length us, event | category | flops | bytes accessed | tf_op | source)
XLA Modules:
  0.0 411.0 jit_solution(6889299718982725748)
XLA Ops:
  3.3 4.5 %collective-permute-start = (f32[1,8,512]{2,1,0:T(8,128)S(1)}, f32[1,8,512]{2,1,0:T(8,128)S(1)}, u32[]{:S(2)}, u32[]{:S(2)}) collective-permute-start(f32[1,8,512]{2,1,0:T(8,128)S(1)} %get-tuple-element.37), channel_id=1, source_target_pairs={{0,8},{8,16},{16,24},{1,9},{9,17},{17,25},{2,10},{10,18},{18,26},{... | collective-permute-start | bytes 49160 | tf_op jit(solution)/shard_map/ppermute | solution.py:17
  7.8 5.9 %copy.46 = s32[4,8,8,512]{2,1,3,0:T(8,128)} copy(s32[4,8,8,512]{3,2,1,0:T(8,128)} %param.32) | data formatting | bytes 1048576 | tf_op args[15]
  13.8 7.3 %add_select_fusion = s32[4,8,8,4,128]{2,1,4,3,0:T(8,128)} fusion(s32[4,8,8,4,128]{2,1,4,3,0:T(8,128)} %bitcast.140), kind=kLoop, calls=%fused_computation.13 | loop fusion | flops 1441792 | bytes 1048576 | tf_op jit(solution)/shard_map/jit(remainder)/select_n | solution.py:63
  26.0 3.4 collective-permute-done.3
  29.9 3.4 collective-permute-start.4
  38.4 4.1 collective-permute-start.6
  47.8 10.4 %select_reduce_fusion.7 = f32[8,32,128]{2,1,0:T(8,128)S(1)} fusion(f32[8,32,128]{2,1,0:T(8,128)S(1)} %fusion.25, s32[8,32,128]{2,1,0:T(8,128)S(1)} %add_select_fusion.8), kind=kLoop, calls=%fused_computation.11 | loop fusion | flops 12550144 | bytes 393216 | tf_op jit(solution)/shard_map/reduce_sum | solution.py:73
  61.0 3.6 collective-permute-start.8
  75.5 3.8 collective-permute-done.11
  85.4 34.5 %select_reduce_fusion.2 = f32[27,32,128]{2,1,0:T(8,128)S(1)} fusion(f32[27,32,128]{2,1,0:T(8,128)S(1)} %fusion.1, s32[27,32,128]{2,1,0:T(8,128)S(1)} %add_select_fusion.4), kind=kLoop, calls=%fused_computation.4 | loop fusion | flops 42356736 | bytes 1327104 | tf_op jit(solution)/shard_map/reduce_sum | solution.py:73
  123.3 5.4 %collective-permute-start.12 = (f32[1,1,1024]{2,1,0:T(1,128)S(1)}, f32[1,1,1024]{2,1,0:T(1,128)S(1)}, u32[]{:S(2)}, u32[]{:S(2)}) collective-permute-start(f32[1,1,1024]{2,1,0:T(1,128)S(1)} %slice.480), channel_id=1, source_target_pairs={{0,8},{8,16},{16,24},{1,9},{9,17},{17,25},{2,10},{10,18},{18,26},{... | collective-permute-start | bytes 12296 | tf_op jit(solution)/shard_map/ppermute | solution.py:17
  131.1 4.7 %collective-permute-start.14 = (f32[3,1,1024]{2,1,0:T(1,128)S(1)}, f32[3,1,1024]{2,1,0:T(1,128)S(1)}, u32[]{:S(2)}, u32[]{:S(2)}) collective-permute-start(f32[3,1,1024]{2,1,0:T(1,128)S(1)} %pad_maximum_fusion.56), channel_id=1, source_target_pairs={{0,1},{1,2},{2,3},{3,4},{4,5},{5,6},{6,7},{8,9},{9,10},{10,11},{11... | collective-permute-start | bytes 36872 | tf_op jit(solution)/shard_map/ppermute | solution.py:17
  137.6 20.8 %select_reduce_fusion.5 = f32[16,32,128]{2,1,0:T(8,128)S(1)} fusion(f32[16,32,128]{2,1,0:T(8,128)S(1)} %fusion.32, s32[16,32,128]{2,1,0:T(8,128)S(1)} %add_select_fusion.6), kind=kLoop, calls=%fused_computation.8 | loop fusion | flops 25100288 | bytes 786432 | tf_op jit(solution)/shard_map/reduce_sum | solution.py:73
  162.4 4.2 %collective-permute-start.16 = (f32[1,1,1024]{2,1,0:T(1,128)S(1)}, f32[1,1,1024]{2,1,0:T(1,128)S(1)}, u32[]{:S(2)}, u32[]{:S(2)}) collective-permute-start(f32[1,1,1024]{2,1,0:T(1,128)S(1)} %slice.483), channel_id=1, source_target_pairs={{0,8},{8,16},{16,24},{1,9},{9,17},{17,25},{2,10},{10,18},{18,26},{... | collective-permute-start | bytes 12296 | tf_op jit(solution)/shard_map/ppermute | solution.py:17
  168.8 5.3 %collective-permute-start.18 = (f32[3,1,1024]{2,1,0:T(1,128)S(1)}, f32[3,1,1024]{2,1,0:T(1,128)S(1)}, u32[]{:S(2)}, u32[]{:S(2)}) collective-permute-start(f32[3,1,1024]{2,1,0:T(1,128)S(1)} %pad_maximum_fusion.57), channel_id=1, source_target_pairs={{0,1},{1,2},{2,3},{3,4},{4,5},{5,6},{6,7},{8,9},{9,10},{10,11},{11... | collective-permute-start | bytes 36872 | tf_op jit(solution)/shard_map/ppermute | solution.py:17
  175.6 20.8 %select_reduce_fusion.4 = f32[16,32,128]{2,1,0:T(8,128)S(1)} fusion(f32[16,32,128]{2,1,0:T(8,128)S(1)} %fusion.30, s32[16,32,128]{2,1,0:T(8,128)S(1)} %add_select_fusion.6), kind=kLoop, calls=%fused_computation.7 | loop fusion | flops 25100288 | bytes 786432 | tf_op jit(solution)/shard_map/reduce_sum | solution.py:73
  200.3 4.5 %collective-permute-start.20 = (f32[1,1,1024]{2,1,0:T(1,128)S(1)}, f32[1,1,1024]{2,1,0:T(1,128)S(1)}, u32[]{:S(2)}, u32[]{:S(2)}) collective-permute-start(f32[1,1,1024]{2,1,0:T(1,128)S(1)} %slice.486), channel_id=1, source_target_pairs={{0,8},{8,16},{16,24},{1,9},{9,17},{17,25},{2,10},{10,18},{18,26},{... | collective-permute-start | bytes 12296 | tf_op jit(solution)/shard_map/ppermute | solution.py:17
  206.9 5.4 %collective-permute-start.22 = (f32[3,1,1024]{2,1,0:T(1,128)S(1)}, f32[3,1,1024]{2,1,0:T(1,128)S(1)}, u32[]{:S(2)}, u32[]{:S(2)}) collective-permute-start(f32[3,1,1024]{2,1,0:T(1,128)S(1)} %pad_maximum_fusion.58), channel_id=1, source_target_pairs={{0,1},{1,2},{2,3},{3,4},{4,5},{5,6},{6,7},{8,9},{9,10},{10,11},{11... | collective-permute-start | bytes 36872 | tf_op jit(solution)/shard_map/ppermute | solution.py:17
  212.4 5.1 %copy.47 = s32[4,8,8,4,128]{4,3,2,1,0:T(4,128)S(1)} copy(s32[4,8,8,4,128]{2,1,4,3,0:T(8,128)} %add_select_fusion) | data formatting | bytes 1048576 | tf_op jit(solution)/shard_map/jit(remainder)/select_n | solution.py:63
  218.1 20.8 %select_reduce_fusion.3 = f32[16,32,128]{2,1,0:T(8,128)S(1)} fusion(f32[16,32,128]{2,1,0:T(8,128)S(1)} %fusion.28, s32[16,32,128]{2,1,0:T(8,128)S(1)} %add_select_fusion.6), kind=kLoop, calls=%fused_computation.6 | loop fusion | flops 25100288 | bytes 786432 | tf_op jit(solution)/shard_map/reduce_sum | solution.py:73
  239.7 41.7 %select_reduce_fusion = f32[4,8,32,128]{3,2,1,0:T(8,128)S(1)} fusion(f32[4,8,32,128]{3,2,1,0:T(8,128)S(1)} %fusion.10, s32[4,8,32,128]{3,2,1,0:T(8,128)S(1)} %copy.54), kind=kLoop, calls=%fused_computation | loop fusion | flops 50200576 | bytes 1572864 | tf_op jit(solution)/shard_map/reduce_sum | solution.py:73
  284.7 4.5 %collective-permute-start.24 = (f32[1,3,4096]{2,1,0:T(4,128)S(1)}, f32[1,3,4096]{2,1,0:T(4,128)S(1)}, u32[]{:S(2)}, u32[]{:S(2)}) collective-permute-start(f32[1,3,4096]{2,1,0:T(4,128)S(1)} %get-tuple-element.27), channel_id=1, source_target_pairs={{0,8},{8,16},{16,24},{1,9},{9,17},{17,25},{2,10},{10,18},{18,26},{... | collective-permute-start | bytes 147464 | tf_op jit(solution)/shard_map/ppermute | solution.py:17
  290.6 41.9 %select_reduce_fusion.1 = f32[4,8,8,4,128]{4,3,2,1,0:T(4,128)S(1)} fusion(f32[4,8,8,4,128]{4,3,2,1,0:T(4,128)S(1)} %fusion.12, s32[4,8,8,4,128]{4,3,2,1,0:T(4,128)S(1)} %copy.47), kind=kLoop, calls=%fused_computation.2 | loop fusion | flops 50200576 | bytes 1572864 | tf_op jit(solution)/shard_map/reduce_sum | solution.py:73
  333.8 4.8 %collective-permute-start.26 = (f32[5,1,4096]{2,1,0:T(1,128)S(1)}, f32[5,1,4096]{2,1,0:T(1,128)S(1)}, u32[]{:S(2)}, u32[]{:S(2)}) collective-permute-start(f32[5,1,4096]{2,1,0:T(1,128)S(1)} %get-tuple-element.2), channel_id=1, source_target_pairs={{0,1},{1,2},{2,3},{3,4},{4,5},{5,6},{6,7},{8,9},{9,10},{10,11},{11... | collective-permute-start | bytes 245768 | tf_op jit(solution)/shard_map/ppermute | solution.py:17
  345.5 11.3 %select_reduce_fusion.6 = f32[8,32,128]{2,1,0:T(8,128)S(1)} fusion(f32[8,32,128]{2,1,0:T(8,128)S(1)} %maximum_select_fusion, s32[8,32,128]{2,1,0:T(8,128)S(1)} %add_select_fusion.8), kind=kLoop, calls=%fused_computation.10 | loop fusion | flops 12550144 | bytes 393216 | tf_op jit(solution)/shard_map/reduce_sum | solution.py:80
  358.0 3.6 collective-permute-start.28
  366.7 4.5 %collective-permute-start.30 = (f32[10,1,512]{2,1,0:T(1,128)S(1)}, f32[10,1,512]{2,1,0:T(1,128)S(1)}, u32[]{:S(2)}, u32[]{:S(2)}) collective-permute-start(f32[10,1,512]{2,1,0:T(1,128)S(1)} %get-tuple-element.14), channel_id=1, source_target_pairs={{0,1},{1,2},{2,3},{3,4},{4,5},{5,6},{6,7},{8,9},{9,10},{10,11},{11... | collective-permute-start | bytes 61448 | tf_op jit(solution)/shard_map/ppermute | solution.py:17
  376.2 3.4 collective-permute-start.32
  384.6 3.6 collective-permute-start.34
  389.6 3.2 collective-permute-done.35
  393.3 3.4 collective-permute-start.36
  401.8 3.6 collective-permute-start.38
  (204 shorter events, 101.4 us)
Async XLA Ops:
  1.4 19.9 %collective-permute-start.1 = (f32[1,8,512]{2,1,0:T(8,128)S(1)}, f32[1,8,512]{2,1,0:T(8,128)S(1)}, u32[]{:S(2)}, u32[]{:S(2)}) collective-permute-start(f32[1,8,512]{2,1,0:T(8,128)S(1)} %get-tuple-element.36), channel_id=1, source_target_pairs={{8,0},{16,8},{24,16},{9,1},{17,9},{25,17},{10,2},{18,10},{26,18},{... | collective-permute-start | bytes 49160 | tf_op jit(solution)/shard_map/ppermute | solution.py:18
  3.3 17.9 %collective-permute-start = (f32[1,8,512]{2,1,0:T(8,128)S(1)}, f32[1,8,512]{2,1,0:T(8,128)S(1)}, u32[]{:S(2)}, u32[]{:S(2)}) collective-permute-start(f32[1,8,512]{2,1,0:T(8,128)S(1)} %get-tuple-element.37), channel_id=1, source_target_pairs={{0,8},{8,16},{16,24},{1,9},{9,17},{17,25},{2,10},{10,18},{18,26},{... | collective-permute-start | bytes 49160 | tf_op jit(solution)/shard_map/ppermute | solution.py:17
  29.9 5.5 %collective-permute-start.4 = (f32[1,8,512]{2,1,0:T(8,128)S(1)}, f32[1,8,512]{2,1,0:T(8,128)S(1)}, u32[]{:S(2)}, u32[]{:S(2)}) collective-permute-start(f32[1,8,512]{2,1,0:T(8,128)S(1)} %get-tuple-element.34), channel_id=1, source_target_pairs={{0,8},{8,16},{16,24},{1,9},{9,17},{17,25},{2,10},{10,18},{18,26},{... | collective-permute-start | bytes 49160 | tf_op jit(solution)/shard_map/ppermute | solution.py:17
  33.3 5.1 %collective-permute-start.5 = (f32[1,8,512]{2,1,0:T(8,128)S(1)}, f32[1,8,512]{2,1,0:T(8,128)S(1)}, u32[]{:S(2)}, u32[]{:S(2)}) collective-permute-start(f32[1,8,512]{2,1,0:T(8,128)S(1)} %get-tuple-element.35), channel_id=1, source_target_pairs={{8,0},{16,8},{24,16},{9,1},{17,9},{25,17},{10,2},{18,10},{26,18},{... | collective-permute-start | bytes 49160 | tf_op jit(solution)/shard_map/ppermute | solution.py:18
  38.4 5.7 %collective-permute-start.6 = (f32[10,1,512]{2,1,0:T(1,128)S(1)}, f32[10,1,512]{2,1,0:T(1,128)S(1)}, u32[]{:S(2)}, u32[]{:S(2)}) collective-permute-start(f32[10,1,512]{2,1,0:T(1,128)S(1)} %get-tuple-element.16), channel_id=1, source_target_pairs={{0,1},{1,2},{2,3},{3,4},{4,5},{5,6},{6,7},{8,9},{9,10},{10,11},{11... | collective-permute-start | bytes 61448 | tf_op jit(solution)/shard_map/ppermute | solution.py:17
  59.0 9.0 %collective-permute-start.9 = (f32[1,3,4096]{2,1,0:T(4,128)}, f32[1,3,4096]{2,1,0:T(4,128)}, u32[]{:S(2)}, u32[]{:S(2)}) collective-permute-start(f32[1,3,4096]{2,1,0:T(4,128)} %get-tuple-element.30), channel_id=1, source_target_pairs={{8,0},{16,8},{24,16},{9,1},{17,9},{25,17},{10,2},{18,10},{26,18},{... | collective-permute-start | bytes 147464 | tf_op jit(solution)/shard_map/ppermute | solution.py:18
  61.0 5.3 %collective-permute-start.8 = (f32[1,3,4096]{2,1,0:T(4,128)}, f32[1,3,4096]{2,1,0:T(4,128)}, u32[]{:S(2)}, u32[]{:S(2)}) collective-permute-start(f32[1,3,4096]{2,1,0:T(4,128)} %get-tuple-element.31), channel_id=1, source_target_pairs={{0,8},{8,16},{16,24},{1,9},{9,17},{17,25},{2,10},{10,18},{18,26},{... | collective-permute-start | bytes 147464 | tf_op jit(solution)/shard_map/ppermute | solution.py:17
  70.4 5.0 %collective-permute-start.10 = (f32[5,1,4096]{2,1,0:T(1,128)}, f32[5,1,4096]{2,1,0:T(1,128)S(1)}, u32[]{:S(2)}, u32[]{:S(2)}) collective-permute-start(f32[5,1,4096]{2,1,0:T(1,128)} %get-tuple-element.4), channel_id=1, source_target_pairs={{0,1},{1,2},{2,3},{3,4},{4,5},{5,6},{6,7},{8,9},{9,10},{10,11},{11... | collective-permute-start | bytes 245768 | tf_op jit(solution)/shard_map/ppermute | solution.py:17
  73.6 5.7 %collective-permute-start.11 = (f32[5,1,4096]{2,1,0:T(1,128)}, f32[5,1,4096]{2,1,0:T(1,128)}, u32[]{:S(2)}, u32[]{:S(2)}) collective-permute-start(f32[5,1,4096]{2,1,0:T(1,128)} %get-tuple-element.5), channel_id=1, source_target_pairs={{1,0},{2,1},{3,2},{4,3},{5,4},{6,5},{7,6},{9,8},{10,9},{11,10},{12... | collective-permute-start | bytes 245768 | tf_op jit(solution)/shard_map/ppermute | solution.py:18
  121.3 8.5 %collective-permute-start.13 = (f32[1,1,1024]{2,1,0:T(1,128)S(1)}, f32[1,1,1024]{2,1,0:T(1,128)S(1)}, u32[]{:S(2)}, u32[]{:S(2)}) collective-permute-start(f32[1,1,1024]{2,1,0:T(1,128)S(1)} %slice.480), channel_id=1, source_target_pairs={{8,0},{16,8},{24,16},{9,1},{17,9},{25,17},{10,2},{18,10},{26,18},{... | collective-permute-start | bytes 12296 | tf_op jit(solution)/shard_map/ppermute | solution.py:18
  123.3 6.5 %collective-permute-start.12 = (f32[1,1,1024]{2,1,0:T(1,128)S(1)}, f32[1,1,1024]{2,1,0:T(1,128)S(1)}, u32[]{:S(2)}, u32[]{:S(2)}) collective-permute-start(f32[1,1,1024]{2,1,0:T(1,128)S(1)} %slice.480), channel_id=1, source_target_pairs={{0,8},{8,16},{16,24},{1,9},{9,17},{17,25},{2,10},{10,18},{18,26},{... | collective-permute-start | bytes 12296 | tf_op jit(solution)/shard_map/ppermute | solution.py:17
  129.8 7.3 %collective-permute-start.15 = (f32[3,1,1024]{2,1,0:T(1,128)S(1)}, f32[3,1,1024]{2,1,0:T(1,128)S(1)}, u32[]{:S(2)}, u32[]{:S(2)}) collective-permute-start(f32[3,1,1024]{2,1,0:T(1,128)S(1)} %pad_maximum_fusion.56), channel_id=1, source_target_pairs={{1,0},{2,1},{3,2},{4,3},{5,4},{6,5},{7,6},{9,8},{10,9},{11,10},{12... | collective-permute-start | bytes 36872 | tf_op jit(solution)/shard_map/ppermute | solution.py:18
  131.1 6.0 %collective-permute-start.14 = (f32[3,1,1024]{2,1,0:T(1,128)S(1)}, f32[3,1,1024]{2,1,0:T(1,128)S(1)}, u32[]{:S(2)}, u32[]{:S(2)}) collective-permute-start(f32[3,1,1024]{2,1,0:T(1,128)S(1)} %pad_maximum_fusion.56), channel_id=1, source_target_pairs={{0,1},{1,2},{2,3},{3,4},{4,5},{5,6},{6,7},{8,9},{9,10},{10,11},{11... | collective-permute-start | bytes 36872 | tf_op jit(solution)/shard_map/ppermute | solution.py:17
  160.4 7.0 %collective-permute-start.17 = (f32[1,1,1024]{2,1,0:T(1,128)S(1)}, f32[1,1,1024]{2,1,0:T(1,128)S(1)}, u32[]{:S(2)}, u32[]{:S(2)}) collective-permute-start(f32[1,1,1024]{2,1,0:T(1,128)S(1)} %slice.483), channel_id=1, source_target_pairs={{8,0},{16,8},{24,16},{9,1},{17,9},{25,17},{10,2},{18,10},{26,18},{... | collective-permute-start | bytes 12296 | tf_op jit(solution)/shard_map/ppermute | solution.py:18
  162.4 5.1 %collective-permute-start.16 = (f32[1,1,1024]{2,1,0:T(1,128)S(1)}, f32[1,1,1024]{2,1,0:T(1,128)S(1)}, u32[]{:S(2)}, u32[]{:S(2)}) collective-permute-start(f32[1,1,1024]{2,1,0:T(1,128)S(1)} %slice.483), channel_id=1, source_target_pairs={{0,8},{8,16},{16,24},{1,9},{9,17},{17,25},{2,10},{10,18},{18,26},{... | collective-permute-start | bytes 12296 | tf_op jit(solution)/shard_map/ppermute | solution.py:17
  167.5 7.6 %collective-permute-start.19 = (f32[3,1,1024]{2,1,0:T(1,128)S(1)}, f32[3,1,1024]{2,1,0:T(1,128)S(1)}, u32[]{:S(2)}, u32[]{:S(2)}) collective-permute-start(f32[3,1,1024]{2,1,0:T(1,128)S(1)} %pad_maximum_fusion.57), channel_id=1, source_target_pairs={{1,0},{2,1},{3,2},{4,3},{5,4},{6,5},{7,6},{9,8},{10,9},{11,10},{12... | collective-permute-start | bytes 36872 | tf_op jit(solution)/shard_map/ppermute | solution.py:18
  168.8 6.3 %collective-permute-start.18 = (f32[3,1,1024]{2,1,0:T(1,128)S(1)}, f32[3,1,1024]{2,1,0:T(1,128)S(1)}, u32[]{:S(2)}, u32[]{:S(2)}) collective-permute-start(f32[3,1,1024]{2,1,0:T(1,128)S(1)} %pad_maximum_fusion.57), channel_id=1, source_target_pairs={{0,1},{1,2},{2,3},{3,4},{4,5},{5,6},{6,7},{8,9},{9,10},{10,11},{11... | collective-permute-start | bytes 36872 | tf_op jit(solution)/shard_map/ppermute | solution.py:17
  198.4 7.1 %collective-permute-start.21 = (f32[1,1,1024]{2,1,0:T(1,128)S(1)}, f32[1,1,1024]{2,1,0:T(1,128)S(1)}, u32[]{:S(2)}, u32[]{:S(2)}) collective-permute-start(f32[1,1,1024]{2,1,0:T(1,128)S(1)} %slice.486), channel_id=1, source_target_pairs={{8,0},{16,8},{24,16},{9,1},{17,9},{25,17},{10,2},{18,10},{26,18},{... | collective-permute-start | bytes 12296 | tf_op jit(solution)/shard_map/ppermute | solution.py:18
  200.3 5.2 %collective-permute-start.20 = (f32[1,1,1024]{2,1,0:T(1,128)S(1)}, f32[1,1,1024]{2,1,0:T(1,128)S(1)}, u32[]{:S(2)}, u32[]{:S(2)}) collective-permute-start(f32[1,1,1024]{2,1,0:T(1,128)S(1)} %slice.486), channel_id=1, source_target_pairs={{0,8},{8,16},{16,24},{1,9},{9,17},{17,25},{2,10},{10,18},{18,26},{... | collective-permute-start | bytes 12296 | tf_op jit(solution)/shard_map/ppermute | solution.py:17
  205.6 12.0 %collective-permute-start.23 = (f32[3,1,1024]{2,1,0:T(1,128)S(1)}, f32[3,1,1024]{2,1,0:T(1,128)S(1)}, u32[]{:S(2)}, u32[]{:S(2)}) collective-permute-start(f32[3,1,1024]{2,1,0:T(1,128)S(1)} %pad_maximum_fusion.58), channel_id=1, source_target_pairs={{1,0},{2,1},{3,2},{4,3},{5,4},{6,5},{7,6},{9,8},{10,9},{11,10},{12... | collective-permute-start | bytes 36872 | tf_op jit(solution)/shard_map/ppermute | solution.py:18
  206.9 10.7 %collective-permute-start.22 = (f32[3,1,1024]{2,1,0:T(1,128)S(1)}, f32[3,1,1024]{2,1,0:T(1,128)S(1)}, u32[]{:S(2)}, u32[]{:S(2)}) collective-permute-start(f32[3,1,1024]{2,1,0:T(1,128)S(1)} %pad_maximum_fusion.58), channel_id=1, source_target_pairs={{0,1},{1,2},{2,3},{3,4},{4,5},{5,6},{6,7},{8,9},{9,10},{10,11},{11... | collective-permute-start | bytes 36872 | tf_op jit(solution)/shard_map/ppermute | solution.py:17
  282.8 50.8 %collective-permute-start.25 = (f32[1,3,4096]{2,1,0:T(4,128)S(1)}, f32[1,3,4096]{2,1,0:T(4,128)S(1)}, u32[]{:S(2)}, u32[]{:S(2)}) collective-permute-start(f32[1,3,4096]{2,1,0:T(4,128)S(1)} %get-tuple-element.26), channel_id=1, source_target_pairs={{8,0},{16,8},{24,16},{9,1},{17,9},{25,17},{10,2},{18,10},{26,18},{... | collective-permute-start | bytes 147464 | tf_op jit(solution)/shard_map/ppermute | solution.py:18
  284.7 48.8 %collective-permute-start.24 = (f32[1,3,4096]{2,1,0:T(4,128)S(1)}, f32[1,3,4096]{2,1,0:T(4,128)S(1)}, u32[]{:S(2)}, u32[]{:S(2)}) collective-permute-start(f32[1,3,4096]{2,1,0:T(4,128)S(1)} %get-tuple-element.27), channel_id=1, source_target_pairs={{0,8},{8,16},{16,24},{1,9},{9,17},{17,25},{2,10},{10,18},{18,26},{... | collective-permute-start | bytes 147464 | tf_op jit(solution)/shard_map/ppermute | solution.py:17
  333.8 7.3 %collective-permute-start.26 = (f32[5,1,4096]{2,1,0:T(1,128)S(1)}, f32[5,1,4096]{2,1,0:T(1,128)S(1)}, u32[]{:S(2)}, u32[]{:S(2)}) collective-permute-start(f32[5,1,4096]{2,1,0:T(1,128)S(1)} %get-tuple-element.2), channel_id=1, source_target_pairs={{0,1},{1,2},{2,3},{3,4},{4,5},{5,6},{6,7},{8,9},{9,10},{10,11},{11... | collective-permute-start | bytes 245768 | tf_op jit(solution)/shard_map/ppermute | solution.py:17
  338.6 5.5 %collective-permute-start.27 = (f32[5,1,4096]{2,1,0:T(1,128)S(1)}, f32[5,1,4096]{2,1,0:T(1,128)S(1)}, u32[]{:S(2)}, u32[]{:S(2)}) collective-permute-start(f32[5,1,4096]{2,1,0:T(1,128)S(1)} %get-tuple-element.3), channel_id=1, source_target_pairs={{1,0},{2,1},{3,2},{4,3},{5,4},{6,5},{7,6},{9,8},{10,9},{11,10},{12... | collective-permute-start | bytes 245768 | tf_op jit(solution)/shard_map/ppermute | solution.py:18
  358.0 5.5 %collective-permute-start.28 = (f32[1,8,512]{2,1,0:T(8,128)S(1)}, f32[1,8,512]{2,1,0:T(8,128)S(1)}, u32[]{:S(2)}, u32[]{:S(2)}) collective-permute-start(f32[1,8,512]{2,1,0:T(8,128)S(1)} %get-tuple-element.24), channel_id=1, source_target_pairs={{0,8},{8,16},{16,24},{1,9},{9,17},{17,25},{2,10},{10,18},{18,26},{... | collective-permute-start | bytes 49160 | tf_op jit(solution)/shard_map/ppermute | solution.py:17
  361.6 5.1 %collective-permute-start.29 = (f32[1,8,512]{2,1,0:T(8,128)S(1)}, f32[1,8,512]{2,1,0:T(8,128)S(1)}, u32[]{:S(2)}, u32[]{:S(2)}) collective-permute-start(f32[1,8,512]{2,1,0:T(8,128)S(1)} %get-tuple-element.25), channel_id=1, source_target_pairs={{8,0},{16,8},{24,16},{9,1},{17,9},{25,17},{10,2},{18,10},{26,18},{... | collective-permute-start | bytes 49160 | tf_op jit(solution)/shard_map/ppermute | solution.py:18
  366.7 5.8 %collective-permute-start.30 = (f32[10,1,512]{2,1,0:T(1,128)S(1)}, f32[10,1,512]{2,1,0:T(1,128)S(1)}, u32[]{:S(2)}, u32[]{:S(2)}) collective-permute-start(f32[10,1,512]{2,1,0:T(1,128)S(1)} %get-tuple-element.14), channel_id=1, source_target_pairs={{0,1},{1,2},{2,3},{3,4},{4,5},{5,6},{6,7},{8,9},{9,10},{10,11},{11... | collective-permute-start | bytes 61448 | tf_op jit(solution)/shard_map/ppermute | solution.py:17
  376.2 5.3 %collective-permute-start.32 = (f32[1,8,512]{2,1,0:T(8,128)S(1)}, f32[1,8,512]{2,1,0:T(8,128)S(1)}, u32[]{:S(2)}, u32[]{:S(2)}) collective-permute-start(f32[1,8,512]{2,1,0:T(8,128)S(1)} %get-tuple-element.22), channel_id=1, source_target_pairs={{0,8},{8,16},{16,24},{1,9},{9,17},{17,25},{2,10},{10,18},{18,26},{... | collective-permute-start | bytes 49160 | tf_op jit(solution)/shard_map/ppermute | solution.py:17
  379.5 5.1 %collective-permute-start.33 = (f32[1,8,512]{2,1,0:T(8,128)S(1)}, f32[1,8,512]{2,1,0:T(8,128)S(1)}, u32[]{:S(2)}, u32[]{:S(2)}) collective-permute-start(f32[1,8,512]{2,1,0:T(8,128)S(1)} %get-tuple-element.23), channel_id=1, source_target_pairs={{8,0},{16,8},{24,16},{9,1},{17,9},{25,17},{10,2},{18,10},{26,18},{... | collective-permute-start | bytes 49160 | tf_op jit(solution)/shard_map/ppermute | solution.py:18
  393.3 5.3 %collective-permute-start.36 = (f32[1,8,512]{2,1,0:T(8,128)S(1)}, f32[1,8,512]{2,1,0:T(8,128)S(1)}, u32[]{:S(2)}, u32[]{:S(2)}) collective-permute-start(f32[1,8,512]{2,1,0:T(8,128)S(1)} %get-tuple-element.20), channel_id=1, source_target_pairs={{0,8},{8,16},{16,24},{1,9},{9,17},{17,25},{2,10},{10,18},{18,26},{... | collective-permute-start | bytes 49160 | tf_op jit(solution)/shard_map/ppermute | solution.py:17
  396.7 5.1 %collective-permute-start.37 = (f32[1,8,512]{2,1,0:T(8,128)S(1)}, f32[1,8,512]{2,1,0:T(8,128)S(1)}, u32[]{:S(2)}, u32[]{:S(2)}) collective-permute-start(f32[1,8,512]{2,1,0:T(8,128)S(1)} %get-tuple-element.21), channel_id=1, source_target_pairs={{8,0},{16,8},{24,16},{9,1},{17,9},{25,17},{10,2},{18,10},{26,18},{... | collective-permute-start | bytes 49160 | tf_op jit(solution)/shard_map/ppermute | solution.py:18
  (24 other events, 696.1 us)
where the time goes:
time: 413 us; the launch traced here: 411 us
  other arithmetic  230 us (56%)
  starting transfers between devices  115 us (28%)
  waiting for transfers between devices  36.1 us (9%)
  local copies, waits for them, and re-layouts  22.1 us (5%)
  matrix products  5.22 us (1%)
    reduce_sum x7, other arithmetic, block_read(): jnp.sum(jnp.where(within, rows[..., None, :], jnp.float32(0.0)), axis=-1)  191 us
    ppermute x20, starting transfers between devices, extended(): before = lax.ppermute(last, axis, up)  82.7 us
    ppermute x20, waiting for transfers between devices, extended(): after = lax.ppermute(first, axis, down)  35.2 us
    ppermute x20, starting transfers between devices, extended(): after = lax.ppermute(first, axis, down)  32.2 us
    reduce_sum x1, other arithmetic, block_add(): jnp.sum(jnp.where(within, grouped[..., None], jnp.float32(0.0)), axis=-2)  11.3 us
    unnamed x45, local copies, waits for them, and re-layouts  8.76 us
    select_n x5, other arithmetic, block_select(): grouped % BLK  8.73 us
  transfers between devices with their start and end apart: 40, of which 13 were waited for; matrix products, arithmetic and copies ran while one was open for 18% of the time, Pallas kernels for 0%

commit v1 on v0

v1 whole, which is shorter than its diff:
```python
import jax
import jax.numpy as jnp
from jax import lax
from jax.experimental import pallas as pl
from jax.experimental.pallas import tpu as pltpu
from jax.sharding import PartitionSpec as P

BLK = 128
OFFSETS = ((-1, -1), (-1, 0), (-1, 1), (0, -1), (0, 1), (1, -1), (1, 0), (1, 1))
SIDES = ((-1, 0), (1, 0), (0, -1), (0, 1))
MESH_ID = pl.DeviceIdType.MESH


def split_two(table):
    high = table.astype(jnp.bfloat16)
    low = (table - high.astype(jnp.float32)).astype(jnp.bfloat16)
    return jnp.concatenate([high, low], axis=1)


def one_hot(base, width):
    ids = lax.broadcasted_iota(jnp.int32, (base.shape[0], width), 1)
    return jnp.where(ids == base, 1.0, 0.0).astype(jnp.bfloat16)


def pick(index, base, table_two):
    both = jnp.dot(
        one_hot(base, table_two.shape[0]), table_two, preferred_element_type=jnp.float32
    )
    rows = both[:, :BLK] + both[:, BLK:]
    return jnp.take_along_axis(rows, index & (BLK - 1), axis=1, mode="promise_in_bounds")


def make_kernel(sizes, shapes):
    na, nb = sizes
    cx, cy, nz = shapes["rhs"]
    zblocks = nz // BLK
    cells = cx * cy
    fine_rows = cells * zblocks
    cap = shapes["send_cell"][1]
    slots = cap // BLK
    kr, crows, _ = shapes["restrict_col"]
    ka = shapes["coarse_col"][0]
    ki = shapes["interp_row"][0]
    rim_rows = 8

    def fine_place(block):
        return (block % zblocks) * cells + block // zblocks

    def kernel(
        rhs_h, diag_h, center_h, faces_h, count_ref, cell_h, rcol_h, rval_h, ccol_h,
        cdiag_h, cval_h, mdiag_h, mval_h, rrow_h, rrval_h, irow_h, ival_h,
        sol_ref, res_ref,
        field, ysend, yrecv, diag, center, faces, cell, rcol, rval, ccol, cdiag, cval,
        mdiag, mval, rrow, rrval, irow, ival, resid, fine_two, choose, sent, received,
        back, returned, coarse, rim, spread,
        in_sem, halo_send, halo_recv, slot_send, slot_recv, back_send, back_recv,
        rim_send, rim_recv,
    ):
        a = lax.axis_index("gx")
        b = lax.axis_index("gy")

        loads = [
            (rhs_h, field.at[0, pl.ds(1, cx)]), (center_h, center), (faces_h, faces),
            (diag_h, diag), (cell_h, cell), (rcol_h, rcol), (rval_h, rval),
            (ccol_h, ccol), (mdiag_h, mdiag), (mval_h, mval), (cdiag_h, cdiag),
            (cval_h, cval), (rrow_h, rrow), (rrval_h, rrval), (irow_h, irow),
            (ival_h, ival),
        ]
        loads = [
            pltpu.make_async_copy(source, target, in_sem.at[n])
            for n, (source, target) in enumerate(loads)
        ]
        for load in loads:
            load.start()

        def there(step):
            dx, dy = step
            checks = []
            if dx < 0:
                checks.append(a > 0)
            if dx > 0:
                checks.append(a < na - 1)
            if dy < 0:
                checks.append(b > 0)
            if dy > 0:
                checks.append(b < nb - 1)
            out = checks[0]
            for check in checks[1:]:
                out = jnp.logical_and(out, check)
            return out

        exists = [there(step) for step in OFFSETS]
        side_exists = [there(step) for step in SIDES]

        barrier = pltpu.get_barrier_semaphore()
        total = jnp.int32(0)
        for d, (dx, dy) in enumerate(OFFSETS):
            @pl.when(exists[d])
            def _():
                pl.semaphore_signal(
                    barrier, inc=1, device_id=(a + dx, b + dy), device_id_type=MESH_ID
                )
            total = total + exists[d].astype(jnp.int32)

        for s in range(4):
            @pl.when(jnp.logical_not(side_exists[s]))
            def _():
                for t in range(5):
                    if s < 2:
                        field[t, 0 if s == 0 else cx + 1] = jnp.zeros((cy, nz), jnp.float32)
                    else:
                        yrecv[t, s - 2] = jnp.zeros((cx, nz), jnp.float32)
        for d in range(8):
            @pl.when(jnp.logical_not(exists[d]))
            def _():
                received[d] = jnp.zeros((slots, BLK), jnp.float32)
                returned[d] = jnp.zeros((slots, BLK), jnp.float32)
                for t in range(3):
                    rim[t, d] = jnp.zeros((rim_rows, BLK), jnp.float32)

        def halo_copy(t, s):
            dx, dy = SIDES[s]
            if s == 0:
                src, dst = field.at[t, 1], field.at[t, cx + 1]
            elif s == 1:
                src, dst = field.at[t, cx], field.at[t, 0]
            else:
                src, dst = ysend.at[t, s - 2], yrecv.at[t, 3 - s]
            return pltpu.make_async_remote_copy(
                src_ref=src, dst_ref=dst, send_sem=halo_send.at[t, s],
                recv_sem=halo_recv.at[t, s ^ 1],
                device_id=(a + dx, b + dy), device_id_type=MESH_ID,
            )

        def halo_arrival(t, s):
            dx, dy = SIDES[s]
            dst = field.at[t, 0 if s == 0 else cx + 1] if s < 2 else yrecv.at[t, s - 2]
            return pltpu.make_async_remote_copy(
                src_ref=dst, dst_ref=dst, send_sem=halo_send.at[t, s],
                recv_sem=halo_recv.at[t, s],
                device_id=(a + dx, b + dy), device_id_type=MESH_ID,
            )

        def start_halo(t):
            for s in range(4):
                @pl.when(side_exists[s])
                def _():
                    halo_copy(t, s).start()

        def wait_halo(t):
            for s in range(4):
                @pl.when(side_exists[s])
                def _():
                    halo_arrival(t, s).wait_recv()

        def eight_copy(src, dst, send_sem, recv_sem, d):
            dx, dy = OFFSETS[d]
            return pltpu.make_async_remote_copy(
                src_ref=src(d), dst_ref=dst(7 - d), send_sem=send_sem(d),
                recv_sem=recv_sem(7 - d),
                device_id=(a + dx, b + dy), device_id_type=MESH_ID,
            )

        def eight_arrival(dst, send_sem, recv_sem, d):
            dx, dy = OFFSETS[d]
            return pltpu.make_async_remote_copy(
                src_ref=dst(d), dst_ref=dst(d), send_sem=send_sem(d), recv_sem=recv_sem(d),
                device_id=(a + dx, b + dy), device_id_type=MESH_ID,
            )

        slot_plan = (
            lambda d: sent.at[d], lambda d: received.at[d],
            lambda d: slot_send.at[d], lambda d: slot_recv.at[d],
        )
        back_plan = (
            lambda d: back.at[d], lambda d: returned.at[d],
            lambda d: back_send.at[d], lambda d: back_recv.at[d],
        )

        def rim_plan(t):
            return (
                lambda d: coarse.at[t, pl.ds(0, rim_rows)], lambda d: rim.at[t, d],
                lambda d: rim_send.at[t, d], lambda d: rim_recv.at[t, d],
            )

        def start_eight(plan):
            for d in range(8):
                @pl.when(exists[d])
                def _():
                    eight_copy(*plan, d).start()

        def wait_eight(plan):
            for d in range(8):
                @pl.when(exists[d])
                def _():
                    eight_arrival(*plan[1:], d).wait_recv()

        row_ids = lax.broadcasted_iota(jnp.int32, (cy, nz), 0)
        lane_ids = lax.broadcasted_iota(jnp.int32, (cy, nz), 1)

        def beside(t, i):
            centre = field[t, i + 1]
            low = jnp.broadcast_to(yrecv[t, 0, i:i + 1, :], (cy, nz))
            high = jnp.broadcast_to(yrecv[t, 1, i:i + 1, :], (cy, nz))
            return centre, [
                field[t, i],
                field[t, i + 2],
                jnp.where(row_ids == 0, low, pltpu.roll(centre, 1, 0)),
                jnp.where(row_ids == cy - 1, high, pltpu.roll(centre, cy - 1, 0)),
                jnp.where(lane_ids == 0, 0.0, pltpu.roll(centre, 1, 1)),
                jnp.where(lane_ids == nz - 1, 0.0, pltpu.roll(centre, nz - 1, 1)),
            ]

        def operator(t, i):
            centre, near = beside(t, i)
            sums = near[0]
            for one in near[1:]:
                sums = sums + one
            return (6.0 + diag[i]) * centre - sums

        def smoother(t, i):
            centre, near = beside(t, i)
            out = center[i] * centre
            for q in range(6):
                out = out + faces[q, i] * near[q]
            return out

        def put(t, i, value):
            field[t, i + 1] = value
            ysend[t, 0, i:i + 1, :] = value[0:1]
            ysend[t, 1, i:i + 1, :] = value[cy - 1:cy]

        loads[0].wait()
        for i in range(cx):
            value = field[0, i + 1]
            ysend[0, 0, i:i + 1, :] = value[0:1]
            ysend[0, 1, i:i + 1, :] = value[cy - 1:cy]
        pl.semaphore_wait(barrier, total)
        start_halo(0)
        for load in loads[1:5]:
            load.wait()

        cell_index = jnp.concatenate(
            [cell[:, s * BLK:(s + 1) * BLK] for s in range(slots)], axis=0
        )
        cell_base = fine_place(cell_index[:, 0:1] // BLK)
        across = jnp.transpose(
            jnp.broadcast_to(cell_base, (8 * slots, BLK)).astype(jnp.float32)
        )[0:1].astype(jnp.int32)
        fine_ids = lax.broadcasted_iota(jnp.int32, (fine_rows, 8 * slots), 0)
        choose[...] = jnp.where(fine_ids == across, 1.0, 0.0).astype(jnp.bfloat16)

        wait_halo(0)
        for i in range(cx):
            put(1, i, smoother(0, i))
        start_halo(1)
        for load in loads[5:]:
            load.wait()

        wait_halo(1)
        for i in range(cx):
            resid[i] = field[0, i + 1] - operator(1, i)
        table = jnp.concatenate(
            [resid[:, :, z * BLK:(z + 1) * BLK].reshape(cells, BLK) for z in range(zblocks)],
            axis=0,
        )
        fine_two[...] = split_two(table)

        picked = pick(cell_index, cell_base, fine_two[...])
        lanes = lax.broadcasted_iota(jnp.int32, (8, BLK), 1)
        for s in range(slots):
            live = lanes + s * BLK < count_ref[...]
            values = jnp.where(live, picked[8 * s:8 * s + 8], 0.0)
            for d in range(8):
                sent[d, s:s + 1, :] = values[d:d + 1]
        start_eight(slot_plan)

        step = 9 if kr % 9 == 0 else 1

        def restrict_some(c, acc):
            index = rcol[pl.ds(c * step, step)].reshape(step * crows, BLK)
            block = index[:, 0:1] // BLK
            base = jnp.where(block < fine_rows, fine_place(block), -1)
            got = pick(index, base, fine_two[...]).reshape(step, crows, BLK)
            return acc + jnp.sum(got * rval[pl.ds(c * step, step)], axis=0)

        rc = lax.fori_loop(
            0, kr // step, restrict_some, jnp.zeros((crows, BLK), jnp.float32)
        )
        wait_eight(slot_plan)
        received_two = split_two(received[...].reshape(8 * slots, BLK))
        index = rcol[:, 0:rim_rows, :].reshape(kr * rim_rows, BLK)
        got = pick(index, index[:, 0:1] // BLK - fine_rows, received_two)
        more = jnp.sum(
            got.reshape(kr, rim_rows, BLK) * rval[:, 0:rim_rows, :], axis=0
        )
        rc = jnp.concatenate([rc[:rim_rows] + more, rc[rim_rows:]], axis=0)

        def coarse_apply(t, vector, diagonal, values):
            coarse[t] = vector
            start_eight(rim_plan(t))
            index = ccol[...].reshape(ka * crows, BLK)
            got = pick(index, index[:, 0:1] // BLK, split_two(vector))
            own = diagonal[...] * vector + jnp.sum(
                got.reshape(ka, crows, BLK) * values[...], axis=0
            )
            wait_eight(rim_plan(t))
            index = ccol[:, 0:rim_rows, :].reshape(ka * rim_rows, BLK)
            got = pick(
                index, index[:, 0:1] // BLK - crows,
                split_two(rim[t].reshape(8 * rim_rows, BLK)),
            )
            more = jnp.sum(
                got.reshape(ka, rim_rows, BLK) * values[:, 0:rim_rows, :], axis=0
            )
            return jnp.concatenate([own[:rim_rows] + more, own[rim_rows:]], axis=0)

        xc1 = coarse_apply(0, rc, mdiag, mval)
        rc2 = rc - coarse_apply(1, xc1, cdiag, cval)
        xc2 = xc1 + coarse_apply(2, rc2, mdiag, mval)
        coarse_two = split_two(xc2)

        group = 8 if slots % 8 == 0 else 1
        for c in range(slots // group):
            parts = [(c * group + g) * BLK for g in range(group)]
            index = jnp.concatenate(
                [rrow[:, :, p:p + BLK].reshape(ki * 8, BLK) for p in parts], axis=0
            )
            got = pick(index, index[:, 0:1] // BLK, coarse_two)
            for g, p in enumerate(parts):
                mine = got[g * ki * 8:(g + 1) * ki * 8].reshape(ki, 8, BLK)
                values = jnp.sum(mine * rrval[:, :, p:p + BLK], axis=0)
                for d in range(8):
                    back[d, c * group + g:c * group + g + 1, :] = values[d:d + 1]
        start_eight(back_plan)

        for z in range(zblocks):
            p = z * BLK
            index = irow[:, :, :, p:p + BLK].reshape(ki * cells, BLK)
            got = pick(index, index[:, 0:1] // BLK, coarse_two)
            got = got.reshape(ki, cx, cy, BLK) * ival[:, :, :, p:p + BLK]
            field[2, 1:cx + 1, :, p:p + BLK] = (
                field[1, 1:cx + 1, :, p:p + BLK] + jnp.sum(got, axis=0)
            )
        wait_eight(back_plan)

        lane_of = lax.broadcasted_iota(jnp.int32, (BLK, BLK), 0)
        pair_row = lax.broadcasted_iota(jnp.int32, (16, BLK), 0) % 8

        def spread_some(s, carry):
            p = pl.multiple_of(s * BLK, BLK)
            values = jnp.concatenate(
                [returned[d, pl.ds(s, 1), :] for d in range(8)], axis=0
            )
            values = jnp.where(lanes + p < count_ref[...], values, 0.0)
            high = values.astype(jnp.bfloat16)
            low = (values - high.astype(jnp.float32)).astype(jnp.bfloat16)
            pair = jnp.concatenate([high, low], axis=0)
            acc = jnp.zeros((16, BLK), jnp.float32)
            for d in range(8):
                within = cell[d:d + 1, pl.ds(p, BLK)] & (BLK - 1)
                place = jnp.where(lane_of == within, 1.0, 0.0).astype(jnp.bfloat16)
                one = lax.dot_general(
                    pair, place, (((1,), (1,)), ((), ())),
                    preferred_element_type=jnp.float32,
                )
                acc = jnp.where(pair_row == d, one, acc)
            spread[pl.ds(pl.multiple_of(s * 8, 8), 8)] = acc[0:8] + acc[8:16]
            return carry

        lax.fori_loop(0, slots, spread_some, 0)
        both = jnp.dot(
            choose[...], split_two(spread[...]), preferred_element_type=jnp.float32
        )
        added = both[:, :BLK] + both[:, BLK:]
        for z in range(zblocks):
            p = z * BLK
            field[2, 1:cx + 1, :, p:p + BLK] = (
                field[2, 1:cx + 1, :, p:p + BLK]
                + added[z * cells:(z + 1) * cells].reshape(cx, cy, BLK)
            )
        for i in range(cx):
            value = field[2, i + 1]
            ysend[2, 0, i:i + 1, :] = value[0:1]
            ysend[2, 1, i:i + 1, :] = value[cy - 1:cy]
        start_halo(2)
        wait_halo(2)

        for i in range(cx):
            put(3, i, field[0, i + 1] - operator(2, i))
        start_halo(3)
        wait_halo(3)
        for i in range(cx):
            value = field[2, i + 1] + smoother(3, i)
            put(4, i, value)
            sol_ref[i] = value
        start_halo(4)
        wait_halo(4)
        for i in range(cx):
            res_ref[i] = field[0, i + 1] - operator(4, i)

        for t in range(5):
            for s in range(4):
                @pl.when(side_exists[s])
                def _():
                    halo_copy(t, s).wait_send()
        for plan in (slot_plan, back_plan, rim_plan(0), rim_plan(1), rim_plan(2)):
            for d in range(8):
                @pl.when(exists[d])
                def _():
                    eight_copy(*plan, d).wait_send()

    f32, i32, bf16 = jnp.float32, jnp.int32, jnp.bfloat16
    vm = pltpu.VMEM
    dma = pltpu.SemaphoreType.DMA
    scratch = [
        vm((5, cx + 2, cy, nz), f32), vm((5, 2, cx, nz), f32), vm((5, 2, cx, nz), f32),
        vm((cx, cy, nz), f32), vm((cx, cy, nz), f32), vm((6, cx, cy, nz), f32),
        vm((8, cap), i32), vm((kr, crows, BLK), i32), vm((kr, crows, BLK), f32),
        vm((ka, crows, BLK), i32), vm((crows, BLK), f32), vm((ka, crows, BLK), f32),
        vm((crows, BLK), f32), vm((ka, crows, BLK), f32),
        vm((ki, 8, cap), i32), vm((ki, 8, cap), f32),
        vm((ki, cx, cy, nz), i32), vm((ki, cx, cy, nz), f32),
        vm((cx, cy, nz), f32), vm((fine_rows, 2 * BLK), bf16),
        vm((fine_rows, 8 * slots), bf16),
        vm((8, slots, BLK), f32), vm((8, slots, BLK), f32),
        vm((8, slots, BLK), f32), vm((8, slots, BLK), f32),
        vm((3, crows, BLK), f32), vm((3, 8, rim_rows, BLK), f32),
        vm((8 * slots, BLK), f32),
        dma((16,)), dma((5, 4)), dma((5, 4)), dma((8,)), dma((8,)), dma((8,)), dma((8,)),
        dma((3, 8)), dma((3, 8)),
    ]
    whole = pl.BlockSpec(memory_space=pltpu.VMEM)
    anywhere = pl.BlockSpec(memory_space=pl.ANY)
    return pl.pallas_call(
        kernel,
        out_shape=(
            jax.ShapeDtypeStruct((cx, cy, nz), f32),
            jax.ShapeDtypeStruct((cx, cy, nz), f32),
        ),
        in_specs=[anywhere] * 4 + [whole] + [anywhere] * 12,
        out_specs=(whole, whole),
        scratch_shapes=scratch,
        compiler_params=pltpu.CompilerParams(
            collective_id=0, has_side_effects=True, vmem_limit_bytes=40 * 1024 * 1024
        ),
        name="vcycle",
    )


def body(
    rhs, diag, smoother_center, smoother_faces, send_count, send_cell, restrict_col,
    restrict_vals, coarse_col, coarse_diag, coarse_vals, csmooth_diag, csmooth_vals,
    remote_row, remote_vals, interp_row, interp_vals,
):
    def rows(array):
        return array.reshape(array.shape[0], -1, BLK)

    cap = send_cell.shape[-1]
    ki = remote_row.shape[0]
    operands = (
        rhs, diag, smoother_center, smoother_faces,
        jnp.broadcast_to(send_count.reshape(8, 1), (8, BLK)),
        send_cell.reshape(8, cap), rows(restrict_col), rows(restrict_vals),
        rows(coarse_col), coarse_diag.reshape(-1, BLK), rows(coarse_vals),
        csmooth_diag.reshape(-1, BLK), rows(csmooth_vals),
        remote_row.reshape(ki, 8, cap), remote_vals.reshape(ki, 8, cap),
        interp_row, interp_vals,
    )
    shapes = {
        "rhs": rhs.shape, "send_cell": (8, cap), "restrict_col": operands[6].shape,
        "coarse_col": operands[8].shape, "interp_row": interp_row.shape,
    }
    sizes = (lax.axis_size("gx"), lax.axis_size("gy"))
    return make_kernel(sizes, shapes)(*operands)


def solution(mesh):
    fine = P("gx", "gy", None)
    listed = P(None, "gx", "gy", None)
    placed = (
        fine, fine, fine, listed, fine, P("gx", "gy", None, None), listed, listed,
        listed, fine, listed, fine, listed,
        P(None, "gx", "gy", None, None), P(None, "gx", "gy", None, None),
        listed, listed,
    )
    return jax.shard_map(
        body, mesh=mesh, in_specs=placed, out_specs=(fine, fine), check_vma=False
    )
```

time: 413 us -> 68.9 us (0.17)
  other arithmetic: 230 us -> 0 us
  starting transfers between devices: 115 us -> 0 us
  Pallas kernels: 0 us -> 50.9 us
  waiting for transfers between devices: 36.1 us -> 0 us
  local copies, waits for them, and re-layouts: 22.1 us -> 16.5 us
  matrix products: 5.22 us -> 0 us
    reduce_sum x14 -> x0, other arithmetic: 209 us -> none  [the longest x7 191 us: block_read(): jnp.sum(jnp.where(within, rows[..., None, :], jnp.float32(0.0)), axis=-1)]
    ppermute x40 -> x0, starting transfers between devices: 115 us -> none  [the longest x20 82.7 us: extended(): before = lax.ppermute(last, axis, up)]
    pallas_call x0 -> x1, Pallas kernels: none -> 50.9 us  [body(): return make_kernel(sizes, shapes)(*operands)]
    ppermute x40 -> x0, waiting for transfers between devices: 36.1 us -> none  [the longest x20 35.2 us: extended(): after = lax.ppermute(first, axis, down)]
    select_n x11 -> x0, other arithmetic: 12.3 us -> none  [the longest x5 8.73 us: block_select(): grouped % BLK]
    unnamed x45 -> x36, local copies, waits for them, and re-layouts: 8.76 us -> 16.5 us
    slice x21 -> x0, local copies, waits for them, and re-layouts: 5.67 us -> none  [the longest x1 2.82 us: slots_to_owners(): return outer_eight(padded[0::2, 0::2])]
    select_n x2 -> x0, local copies, waits for them, and re-layouts: 5.24 us -> none  [block_select(): grouped % BLK]
  transfers between devices with their start and end apart: 40 -> 0, of which waited for: 13 -> 0; matrix products, arithmetic and copies ran while one was open for 18% -> 0% of each run, Pallas kernels for 0% -> 0%
where the time goes in v1:
time: 68.9 us; the launch traced here: 68.2 us
  Pallas kernels  50.9 us (74%)
  local copies, waits for them, and re-layouts  16.5 us (24%)
    pallas_call x1, Pallas kernels, body(): return make_kernel(sizes, shapes)(*operands)  50.9 us
    unnamed x36, local copies, waits for them, and re-layouts  16.5 us

profile of v1, /device:TPU:1, one launch (start us, length us, event | category | flops | bytes accessed | tf_op | source)
XLA Modules:
  0.0 68.2 jit_solution(16289158722473113597)
XLA Ops:
  0.6 0.0 copy-start.14
  0.6 0.0 copy-start.16
  0.6 0.7 copy-done.16
  1.3 0.1 broadcast_in_dim.8.count_ref
  1.4 0.0 copy-done.14
  1.4 0.0 copy-start
  1.4 1.1 %copy-done = f32[6,8,8,512]{3,2,1,0:T(8,128)S(1)} copy-done((f32[6,8,8,512]{3,2,1,0:T(8,128)S(1)}, f32[6,8,8,512]{3,2,1,0:T(8,128)}, u32[]{:S(2)}) %copy-start) | copy-done | bytes 786456
  2.5 0.0 copy-start.1
  2.5 1.0 %copy-done.1 = s32[4,1,1,8,4096]{4,3,2,1,0:T(8,128)S(1)} copy-done((s32[4,1,1,8,4096]{4,3,2,1,0:T(8,128)S(1)}, s32[4,1,1,8,4096]{4,3,2,1,0:T(8,128)}, u32[]{:S(2)}) %copy-start.1) | copy-done | bytes 524312
  3.6 0.0 copy-start.2
  3.6 1.0 %copy-done.2 = f32[4,1,1,8,4096]{4,3,2,1,0:T(8,128)S(1)} copy-done((f32[4,1,1,8,4096]{4,3,2,1,0:T(8,128)S(1)}, f32[4,1,1,8,4096]{4,3,2,1,0:T(8,128)}, u32[]{:S(2)}) %copy-start.2) | copy-done | bytes 524312
  4.6 0.0 copy-start.3
  4.6 1.0 %copy-done.3 = s32[4,8,8,512]{3,2,1,0:T(8,128)S(1)} copy-done((s32[4,8,8,512]{3,2,1,0:T(8,128)S(1)}, s32[4,8,8,512]{3,2,1,0:T(8,128)}, u32[]{:S(2)}) %copy-start.3) | copy-done | bytes 524312
  5.6 0.0 copy-start.4
  5.6 1.0 %copy-done.4 = f32[4,8,8,512]{3,2,1,0:T(8,128)S(1)} copy-done((f32[4,8,8,512]{3,2,1,0:T(8,128)S(1)}, f32[4,8,8,512]{3,2,1,0:T(8,128)}, u32[]{:S(2)}) %copy-start.4) | copy-done | bytes 524312
  6.7 0.0 copy-start.5
  6.7 1.0 %copy-done.5 = s32[27,1,1,4096]{3,2,1,0:T(1,128)S(1)} copy-done((s32[27,1,1,4096]{3,2,1,0:T(1,128)S(1)}, s32[27,1,1,4096]{3,2,1,0:T(1,128)}, u32[]{:S(2)}) %copy-start.5) | copy-done | bytes 442392
  7.7 0.0 copy-start.6
  7.7 1.0 %copy-done.6 = f32[27,1,1,4096]{3,2,1,0:T(1,128)S(1)} copy-done((f32[27,1,1,4096]{3,2,1,0:T(1,128)S(1)}, f32[27,1,1,4096]{3,2,1,0:T(1,128)}, u32[]{:S(2)}) %copy-start.6) | copy-done | bytes 442392
  8.7 0.0 copy-start.7
  8.7 0.9 %copy-done.7 = s32[16,1,1,4096]{3,2,1,0:T(1,128)S(1)} copy-done((s32[16,1,1,4096]{3,2,1,0:T(1,128)S(1)}, s32[16,1,1,4096]{3,2,1,0:T(1,128)}, u32[]{:S(2)}) %copy-start.7) | copy-done | bytes 262168
  9.7 0.0 copy-start.8
  9.7 0.9 %copy-done.8 = f32[16,1,1,4096]{3,2,1,0:T(1,128)S(1)} copy-done((f32[16,1,1,4096]{3,2,1,0:T(1,128)S(1)}, f32[16,1,1,4096]{3,2,1,0:T(1,128)}, u32[]{:S(2)}) %copy-start.8) | copy-done | bytes 262168
  10.6 0.9 %copy-done.9 = f32[16,1,1,4096]{3,2,1,0:T(1,128)S(1)} copy-done((f32[16,1,1,4096]{3,2,1,0:T(1,128)S(1)}, f32[16,1,1,4096]{3,2,1,0:T(1,128)}, u32[]{:S(2)}) %copy-start.9) | copy-done | bytes 262168
  11.6 0.9 %copy-done.10 = f32[8,8,512]{2,1,0:T(8,128)S(1)} copy-done((f32[8,8,512]{2,1,0:T(8,128)S(1)}, f32[8,8,512]{2,1,0:T(8,128)}, u32[]{:S(2)}) %copy-start.10) | copy-done | bytes 131096
  12.5 0.9 %copy-done.11 = f32[8,8,512]{2,1,0:T(8,128)S(1)} copy-done((f32[8,8,512]{2,1,0:T(8,128)S(1)}, f32[8,8,512]{2,1,0:T(8,128)}, u32[]{:S(2)}) %copy-start.11) | copy-done | bytes 131096
  13.4 0.9 %copy-done.12 = f32[8,8,512]{2,1,0:T(8,128)S(1)} copy-done((f32[8,8,512]{2,1,0:T(8,128)S(1)}, f32[8,8,512]{2,1,0:T(8,128)}, u32[]{:S(2)}) %copy-start.12) | copy-done | bytes 131096
  14.3 0.9 %copy-done.13 = s32[1,1,8,4096]{3,2,1,0:T(8,128)S(1)} copy-done((s32[1,1,8,4096]{3,2,1,0:T(8,128)S(1)}, s32[1,1,8,4096]{3,2,1,0:T(8,128)}, u32[]{:S(2)}) %copy-start.13) | copy-done | bytes 131096
  15.2 0.7 %copy-done.15 = f32[1,1,4096]{2,1,0:T(1,128)S(1)} copy-done((f32[1,1,4096]{2,1,0:T(1,128)S(1)}, f32[1,1,4096]{2,1,0:T(1,128)}, u32[]{:S(2)}) %copy-start.15) | copy-done | bytes 16408
  15.9 50.9 %vcycle.1 = (f32[8,8,512]{2,1,0:T(8,128)S(1)}, f32[8,8,512]{2,1,0:T(8,128)S(1)}) custom-call(f32[8,8,512]{2,1,0:T(8,128)S(1)} %copy-done.10, f32[8,8,512]{2,1,0:T(8,128)S(1)} %copy-done.11, f32[8,8,512]{2,1,0:T(8,128)S(1)} %copy-done.12, f32[6,8,8,512]{3,2,1,0:T(8,128)S(1)} %copy-done, s32[8,128]{1,0:T(8,128)S(1)} %broadcast_in_dim.8.count_ref, ...), custom_call_target="tpu_custom_call" | custom-call | tf_op jit(solution)/shard_map/vcycle/pallas_call | solution.py:475
  66.8 0.7 copy.21
  67.5 0.7 copy.22
  (6 shorter events, 0.0 us)
Async XLA Ops:
  0.6 0.7 %copy-start.14 = (f32[1,1,4096]{2,1,0:T(1,128)S(1)}, f32[1,1,4096]{2,1,0:T(1,128)}, u32[]{:S(2)}) copy-start(f32[1,1,4096]{2,1,0:T(1,128)} %param.26) | copy-start | bytes 49156
  0.6 0.7 copy-start.16
  1.4 1.1 %copy-start = (f32[6,8,8,512]{3,2,1,0:T(8,128)S(1)}, f32[6,8,8,512]{3,2,1,0:T(8,128)}, u32[]{:S(2)}) copy-start(f32[6,8,8,512]{3,2,1,0:T(8,128)} %faces_h.1) | copy-start | bytes 2359300
  2.5 1.0 %copy-start.1 = (s32[4,1,1,8,4096]{4,3,2,1,0:T(8,128)S(1)}, s32[4,1,1,8,4096]{4,3,2,1,0:T(8,128)}, u32[]{:S(2)}) copy-start(s32[4,1,1,8,4096]{4,3,2,1,0:T(8,128)} %param.30) | copy-start | bytes 1572868
  3.6 1.0 %copy-start.2 = (f32[4,1,1,8,4096]{4,3,2,1,0:T(8,128)S(1)}, f32[4,1,1,8,4096]{4,3,2,1,0:T(8,128)}, u32[]{:S(2)}) copy-start(f32[4,1,1,8,4096]{4,3,2,1,0:T(8,128)} %param.31) | copy-start | bytes 1572868
  4.6 1.0 %copy-start.3 = (s32[4,8,8,512]{3,2,1,0:T(8,128)S(1)}, s32[4,8,8,512]{3,2,1,0:T(8,128)}, u32[]{:S(2)}) copy-start(s32[4,8,8,512]{3,2,1,0:T(8,128)} %irow_h.1) | copy-start | bytes 1572868
  5.6 1.0 %copy-start.4 = (f32[4,8,8,512]{3,2,1,0:T(8,128)S(1)}, f32[4,8,8,512]{3,2,1,0:T(8,128)}, u32[]{:S(2)}) copy-start(f32[4,8,8,512]{3,2,1,0:T(8,128)} %ival_h.1) | copy-start | bytes 1572868
  6.7 1.0 %copy-start.5 = (s32[27,1,1,4096]{3,2,1,0:T(1,128)S(1)}, s32[27,1,1,4096]{3,2,1,0:T(1,128)}, u32[]{:S(2)}) copy-start(s32[27,1,1,4096]{3,2,1,0:T(1,128)} %param.23) | copy-start | bytes 1327108
  7.7 1.0 %copy-start.6 = (f32[27,1,1,4096]{3,2,1,0:T(1,128)S(1)}, f32[27,1,1,4096]{3,2,1,0:T(1,128)}, u32[]{:S(2)}) copy-start(f32[27,1,1,4096]{3,2,1,0:T(1,128)} %param.24) | copy-start | bytes 1327108
  8.7 0.9 %copy-start.7 = (s32[16,1,1,4096]{3,2,1,0:T(1,128)S(1)}, s32[16,1,1,4096]{3,2,1,0:T(1,128)}, u32[]{:S(2)}) copy-start(s32[16,1,1,4096]{3,2,1,0:T(1,128)} %param.25) | copy-start | bytes 786436
  9.7 0.9 %copy-start.8 = (f32[16,1,1,4096]{3,2,1,0:T(1,128)S(1)}, f32[16,1,1,4096]{3,2,1,0:T(1,128)}, u32[]{:S(2)}) copy-start(f32[16,1,1,4096]{3,2,1,0:T(1,128)} %param.27) | copy-start | bytes 786436
  10.6 0.9 %copy-start.9 = (f32[16,1,1,4096]{3,2,1,0:T(1,128)S(1)}, f32[16,1,1,4096]{3,2,1,0:T(1,128)}, u32[]{:S(2)}) copy-start(f32[16,1,1,4096]{3,2,1,0:T(1,128)} %param.29) | copy-start | bytes 786436
  11.6 0.9 %copy-start.10 = (f32[8,8,512]{2,1,0:T(8,128)S(1)}, f32[8,8,512]{2,1,0:T(8,128)}, u32[]{:S(2)}) copy-start(f32[8,8,512]{2,1,0:T(8,128)} %rhs_h.1) | copy-start | bytes 393220
  12.5 0.9 %copy-start.11 = (f32[8,8,512]{2,1,0:T(8,128)S(1)}, f32[8,8,512]{2,1,0:T(8,128)}, u32[]{:S(2)}) copy-start(f32[8,8,512]{2,1,0:T(8,128)} %diag_h.1) | copy-start | bytes 393220
  13.4 0.9 %copy-start.12 = (f32[8,8,512]{2,1,0:T(8,128)S(1)}, f32[8,8,512]{2,1,0:T(8,128)}, u32[]{:S(2)}) copy-start(f32[8,8,512]{2,1,0:T(8,128)} %center_h.1) | copy-start | bytes 393220
  14.3 0.9 %copy-start.13 = (s32[1,1,8,4096]{3,2,1,0:T(8,128)S(1)}, s32[1,1,8,4096]{3,2,1,0:T(8,128)}, u32[]{:S(2)}) copy-start(s32[1,1,8,4096]{3,2,1,0:T(8,128)} %param.22) | copy-start | bytes 393220
  15.2 0.7 %copy-start.15 = (f32[1,1,4096]{2,1,0:T(1,128)S(1)}, f32[1,1,4096]{2,1,0:T(1,128)}, u32[]{:S(2)}) copy-start(f32[1,1,4096]{2,1,0:T(1,128)} %param.28) | copy-start | bytes 49156

commit v2 on v1

--- a/solution.py
+++ b/solution.py
@@ -344,8 +344,10 @@
             )
         wait_eight(back_plan)
 
-        lane_of = lax.broadcasted_iota(jnp.int32, (BLK, BLK), 0)
-        pair_row = lax.broadcasted_iota(jnp.int32, (16, BLK), 0) % 8
+        fold_rows = lax.broadcasted_iota(jnp.int32, (64, BLK), 0)
+        fold_lanes = lax.broadcasted_iota(jnp.int32, (64, BLK), 1)
+        fold_index = (fold_lanes % 16) * 8 + fold_rows % 8
+        fold_keep = fold_lanes // 16 == fold_rows // 8
 
         def spread_some(s, carry):
             p = pl.multiple_of(s * BLK, BLK)
@@ -353,22 +355,28 @@
                 [returned[d, pl.ds(s, 1), :] for d in range(8)], axis=0
             )
             values = jnp.where(lanes + p < count_ref[...], values, 0.0)
-            high = values.astype(jnp.bfloat16)
-            low = (values - high.astype(jnp.float32)).astype(jnp.bfloat16)
-            pair = jnp.concatenate([high, low], axis=0)
-            acc = jnp.zeros((16, BLK), jnp.float32)
-            for d in range(8):
-                within = cell[d:d + 1, pl.ds(p, BLK)] & (BLK - 1)
-                place = jnp.where(lane_of == within, 1.0, 0.0).astype(jnp.bfloat16)
-                one = lax.dot_general(
-                    pair, place, (((1,), (1,)), ((), ())),
-                    preferred_element_type=jnp.float32,
-                )
-                acc = jnp.where(pair_row == d, one, acc)
-            spread[pl.ds(pl.multiple_of(s * 8, 8), 8)] = acc[0:8] + acc[8:16]
+            within = cell[:, pl.ds(p, BLK)] & (BLK - 1)
+            upper, lower = within // 16, within % 16
+            coarse_part = jnp.concatenate(
+                [jnp.where(upper == h, values, 0.0) for h in range(8)], axis=0
+            )
+            high = coarse_part.astype(jnp.bfloat16)
+            low = (coarse_part - high.astype(jnp.float32)).astype(jnp.bfloat16)
+            fine_part = jnp.concatenate(
+                [jnp.where(lower == l, 1.0, 0.0) for l in range(16)], axis=0
+            ).astype(jnp.bfloat16)
+            out = lax.dot_general(
+                jnp.concatenate([high, low], axis=0), fine_part,
+                (((1,), (1,)), ((), ())), preferred_element_type=jnp.float32,
+            )
+            out = jnp.take_along_axis(
+                out[:64] + out[64:], fold_index, axis=1, mode="promise_in_bounds"
+            )
+            out = jnp.where(fold_keep, out, 0.0).reshape(8, 8, BLK)
+            spread[pl.ds(pl.multiple_of(s * 8, 8), 8)] = jnp.sum(out, axis=0)
             return carry
 
-        lax.fori_loop(0, slots, spread_some, 0)
+        lax.fori_loop(0, slots, spread_some, 0, unroll=32)
         both = jnp.dot(
             choose[...], split_two(spread[...]), preferred_element_type=jnp.float32
         )
@@ -431,14 +439,14 @@
         dma((3, 8)), dma((3, 8)),
     ]
     whole = pl.BlockSpec(memory_space=pltpu.VMEM)
-    anywhere = pl.BlockSpec(memory_space=pl.ANY)
+    in_hbm = pl.BlockSpec(memory_space=pltpu.HBM)
     return pl.pallas_call(
         kernel,
         out_shape=(
             jax.ShapeDtypeStruct((cx, cy, nz), f32),
             jax.ShapeDtypeStruct((cx, cy, nz), f32),
         ),
-        in_specs=[anywhere] * 4 + [whole] + [anywhere] * 12,
+        in_specs=[in_hbm] * 4 + [whole] + [in_hbm] * 12,
         out_specs=(whole, whole),
         scratch_shapes=scratch,
         compiler_params=pltpu.CompilerParams(
@@ -458,6 +466,9 @@
 
     cap = send_cell.shape[-1]
     ki = remote_row.shape[0]
+    def in_hbm(array):
+        return pltpu.with_memory_space_constraint(array, pltpu.HBM)
+
     operands = (
         rhs, diag, smoother_center, smoother_faces,
         jnp.broadcast_to(send_count.reshape(8, 1), (8, BLK)),
@@ -472,6 +483,7 @@
         "coarse_col": operands[8].shape, "interp_row": interp_row.shape,
     }
     sizes = (lax.axis_size("gx"), lax.axis_size("gy"))
+    operands = [x if n == 4 else in_hbm(x) for n, x in enumerate(operands)]
     return make_kernel(sizes, shapes)(*operands)
 
 

time: 68.9 us -> 45.1 us (0.65)
  local copies, waits for them, and re-layouts: 16.5 us -> 2.03 us
  Pallas kernels: 50.9 us -> 42.3 us
    unnamed x36 -> x4, local copies, waits for them, and re-layouts: 16.5 us -> 1.96 us
    pallas_call x1, Pallas kernels: 50.9 us -> 42.3 us  [body(): return make_kernel(sizes, shapes)(*operands)]
where the time goes in v2:
time: 45.1 us; the launch traced here: 44.9 us
  Pallas kernels  42.3 us (94%)
  local copies, waits for them, and re-layouts  2.03 us (5%)
  between operations  0.65 us (1%)
    pallas_call x1, Pallas kernels, body(): return make_kernel(sizes, shapes)(*operands)  42.3 us
    unnamed x4, local copies, waits for them, and re-layouts  1.96 us

profile of v2, /device:TPU:1, one launch (start us, length us, event | category | flops | bytes accessed | tf_op | source)
XLA Modules:
  0.0 44.9 jit_solution(7630909817990151594)
XLA Ops:
  0.6 0.0 copy-start
  0.6 0.6 %copy-done = s32[1,1,8]{2,1,0:T(1,128)S(1)} copy-done((s32[1,1,8]{2,1,0:T(1,128)S(1)}, s32[1,1,8]{2,1,0:T(1,128)}, u32[]{:S(2)}) %copy-start) | copy-done | bytes 56
  1.3 0.1 broadcast_in_dim.8.count_ref
  1.4 42.3 %vcycle.1 = (f32[8,8,512]{2,1,0:T(8,128)S(1)}, f32[8,8,512]{2,1,0:T(8,128)S(1)}) custom-call(f32[8,8,512]{2,1,0:T(8,128)} %rhs_h.1, f32[8,8,512]{2,1,0:T(8,128)} %diag_h.1, f32[8,8,512]{2,1,0:T(8,128)} %center_h.1, f32[6,8,8,512]{3,2,1,0:T(8,128)} %faces_h.1, s32[8,128]{1,0:T(8,128)S(1)} %broadcast_in_dim.8.count_ref, s32[8,4096]{1,0:T(8,128)} %bitcast.18, ...), custom_call_target="tpu_custom_call" | custom-call | tf_op jit(solution)/shard_map/vcycle/pallas_call | solution.py:487
  43.6 0.7 %copy.21 = f32[8,8,512]{2,1,0:T(8,128)} copy(f32[8,8,512]{2,1,0:T(8,128)S(1)} %get-tuple-element.4) | data formatting | bytes 262144
  44.3 0.7 %copy.22 = f32[8,8,512]{2,1,0:T(8,128)} copy(f32[8,8,512]{2,1,0:T(8,128)S(1)} %get-tuple-element.5) | data formatting | bytes 262144
Async XLA Ops:
  0.6 0.7 %copy-start = (s32[1,1,8]{2,1,0:T(1,128)S(1)}, s32[1,1,8]{2,1,0:T(1,128)}, u32[]{:S(2)}) copy-start(s32[1,1,8]{2,1,0:T(1,128)} %param.21) | copy-start | bytes 100

commit v3 on v2

--- a/solution.py
+++ b/solution.py
@@ -52,7 +52,7 @@
         sol_ref, res_ref,
         field, ysend, yrecv, diag, center, faces, cell, rcol, rval, ccol, cdiag, cval,
         mdiag, mval, rrow, rrval, irow, ival, resid, fine_two, choose, sent, received,
-        back, returned, coarse, rim, spread,
+        back, returned, coarse, rim, spread, partial,
         in_sem, halo_send, halo_recv, slot_send, slot_recv, back_send, back_recv,
         rim_send, rim_recv,
     ):
@@ -142,7 +142,7 @@
             )
 
         def start_halo(t):
-            for s in range(4):
+            for s in (2, 3, 0, 1):
                 @pl.when(side_exists[s])
                 def _():
                     halo_copy(t, s).start()
@@ -184,7 +184,7 @@
             )
 
         def start_eight(plan):
-            for d in range(8):
+            for d in (0, 2, 5, 7, 3, 4, 1, 6):
                 @pl.when(exists[d])
                 def _():
                     eight_copy(*plan, d).start()
@@ -198,31 +198,57 @@
         row_ids = lax.broadcasted_iota(jnp.int32, (cy, nz), 0)
         lane_ids = lax.broadcasted_iota(jnp.int32, (cy, nz), 1)
 
+        zeros = jnp.zeros((cy, nz), jnp.float32)
+
         def beside(t, i):
             centre = field[t, i + 1]
-            low = jnp.broadcast_to(yrecv[t, 0, i:i + 1, :], (cy, nz))
-            high = jnp.broadcast_to(yrecv[t, 1, i:i + 1, :], (cy, nz))
             return centre, [
-                field[t, i],
-                field[t, i + 2],
-                jnp.where(row_ids == 0, low, pltpu.roll(centre, 1, 0)),
-                jnp.where(row_ids == cy - 1, high, pltpu.roll(centre, cy - 1, 0)),
+                field[t, i] if i > 0 else zeros,
+                field[t, i + 2] if i < cx - 1 else zeros,
+                jnp.where(row_ids == 0, 0.0, pltpu.roll(centre, 1, 0)),
+                jnp.where(row_ids == cy - 1, 0.0, pltpu.roll(centre, cy - 1, 0)),
                 jnp.where(lane_ids == 0, 0.0, pltpu.roll(centre, 1, 1)),
                 jnp.where(lane_ids == nz - 1, 0.0, pltpu.roll(centre, nz - 1, 1)),
             ]
 
-        def operator(t, i):
-            centre, near = beside(t, i)
-            sums = near[0]
-            for one in near[1:]:
-                sums = sums + one
-            return (6.0 + diag[i]) * centre - sums
-
-        def smoother(t, i):
-            centre, near = beside(t, i)
-            out = center[i] * centre
-            for q in range(6):
-                out = out + faces[q, i] * near[q]
+        def sides(t, i):
+            out = [
+                jnp.where(row_ids == 0, jnp.broadcast_to(yrecv[t, 0, i:i + 1, :], (cy, nz)), 0.0),
+                jnp.where(row_ids == cy - 1, jnp.broadcast_to(yrecv[t, 1, i:i + 1, :], (cy, nz)), 0.0),
+            ]
+            return [
+                field[t, 0] if i == 0 else None,
+                field[t, cx + 1] if i == cx - 1 else None,
+            ] + out
+
+        def residual_inside(t):
+            for i in range(cx):
+                centre, near = beside(t, i)
+                sums = near[0]
+                for one in near[1:]:
+                    sums = sums + one
+                partial[i] = field[0, i + 1] - ((6.0 + diag[i]) * centre - sums)
+
+        def residual_row(t, i):
+            out = partial[i]
+            for one in sides(t, i):
+                if one is not None:
+                    out = out + one
+            return out
+
+        def smoother_inside(t, base):
+            for i in range(cx):
+                centre, near = beside(t, i)
+                out = center[i] * centre
+                for q in range(6):
+                    out = out + faces[q, i] * near[q]
+                partial[i] = out if base is None else field[base, i + 1] + out
+
+        def smoother_row(t, i):
+            out = partial[i]
+            for q, one in enumerate(sides(t, i)):
+                if one is not None:
+                    out = out + faces[q, i] * one
             return out
 
         def put(t, i, value):
@@ -250,16 +276,18 @@
         fine_ids = lax.broadcasted_iota(jnp.int32, (fine_rows, 8 * slots), 0)
         choose[...] = jnp.where(fine_ids == across, 1.0, 0.0).astype(jnp.bfloat16)
 
+        smoother_inside(0, None)
         wait_halo(0)
         for i in range(cx):
-            put(1, i, smoother(0, i))
+            put(1, i, smoother_row(0, i))
         start_halo(1)
+        residual_inside(1)
         for load in loads[5:]:
             load.wait()
 
         wait_halo(1)
         for i in range(cx):
-            resid[i] = field[0, i + 1] - operator(1, i)
+            resid[i] = residual_row(1, i)
         table = jnp.concatenate(
             [resid[:, :, z * BLK:(z + 1) * BLK].reshape(cells, BLK) for z in range(zblocks)],
             axis=0,
@@ -392,20 +420,23 @@
             ysend[2, 0, i:i + 1, :] = value[0:1]
             ysend[2, 1, i:i + 1, :] = value[cy - 1:cy]
         start_halo(2)
+        residual_inside(2)
         wait_halo(2)
 
         for i in range(cx):
-            put(3, i, field[0, i + 1] - operator(2, i))
+            put(3, i, residual_row(2, i))
         start_halo(3)
+        smoother_inside(3, 2)
         wait_halo(3)
         for i in range(cx):
-            value = field[2, i + 1] + smoother(3, i)
+            value = smoother_row(3, i)
             put(4, i, value)
             sol_ref[i] = value
         start_halo(4)
+        residual_inside(4)
         wait_halo(4)
         for i in range(cx):
-            res_ref[i] = field[0, i + 1] - operator(4, i)
+            res_ref[i] = residual_row(4, i)
 
         for t in range(5):
             for s in range(4):
@@ -434,7 +465,7 @@
         vm((8, slots, BLK), f32), vm((8, slots, BLK), f32),
         vm((8, slots, BLK), f32), vm((8, slots, BLK), f32),
         vm((3, crows, BLK), f32), vm((3, 8, rim_rows, BLK), f32),
-        vm((8 * slots, BLK), f32),
+        vm((8 * slots, BLK), f32), vm((cx, cy, nz), f32),
         dma((16,)), dma((5, 4)), dma((5, 4)), dma((8,)), dma((8,)), dma((8,)), dma((8,)),
         dma((3, 8)), dma((3, 8)),
     ]

time: 45.1 us -> 44.4 us (0.984)
  Pallas kernels: 42.3 us -> 41.5 us
    pallas_call x1, Pallas kernels: 42.3 us -> 41.5 us  [body(): return make_kernel(sizes, shapes)(*operands)]
where the time goes in v3:
time: 44.4 us; the launch traced here: 44.2 us
  Pallas kernels  41.5 us (93%)
  local copies, waits for them, and re-layouts  2.03 us (5%)
  between operations  0.65 us (1%)
    pallas_call x1, Pallas kernels, body(): return make_kernel(sizes, shapes)(*operands)  41.5 us
    unnamed x4, local copies, waits for them, and re-layouts  1.96 us

profile of v3, /device:TPU:1, one launch (start us, length us, event | category | flops | bytes accessed | tf_op | source)
XLA Modules:
  0.0 44.2 jit_solution(3721589901839292966)
XLA Ops:
  0.6 0.0 copy-start
  0.6 0.6 %copy-done = s32[1,1,8]{2,1,0:T(1,128)S(1)} copy-done((s32[1,1,8]{2,1,0:T(1,128)S(1)}, s32[1,1,8]{2,1,0:T(1,128)}, u32[]{:S(2)}) %copy-start) | copy-done | bytes 56
  1.3 0.1 broadcast_in_dim.8.count_ref
  1.4 41.5 %vcycle.1 = (f32[8,8,512]{2,1,0:T(8,128)S(1)}, f32[8,8,512]{2,1,0:T(8,128)S(1)}) custom-call(f32[8,8,512]{2,1,0:T(8,128)} %rhs_h.1, f32[8,8,512]{2,1,0:T(8,128)} %diag_h.1, f32[8,8,512]{2,1,0:T(8,128)} %center_h.1, f32[6,8,8,512]{3,2,1,0:T(8,128)} %faces_h.1, s32[8,128]{1,0:T(8,128)S(1)} %broadcast_in_dim.8.count_ref, s32[8,4096]{1,0:T(8,128)} %bitcast.18, ...), custom_call_target="tpu_custom_call" | custom-call | tf_op jit(solution)/shard_map/vcycle/pallas_call | solution.py:518
  42.9 0.7 %copy.21 = f32[8,8,512]{2,1,0:T(8,128)} copy(f32[8,8,512]{2,1,0:T(8,128)S(1)} %get-tuple-element.4) | data formatting | bytes 262144
  43.6 0.7 %copy.22 = f32[8,8,512]{2,1,0:T(8,128)} copy(f32[8,8,512]{2,1,0:T(8,128)S(1)} %get-tuple-element.5) | data formatting | bytes 262144
Async XLA Ops:
  0.6 0.7 %copy-start = (s32[1,1,8]{2,1,0:T(1,128)S(1)}, s32[1,1,8]{2,1,0:T(1,128)}, u32[]{:S(2)}) copy-start(s32[1,1,8]{2,1,0:T(1,128)} %param.21) | copy-start | bytes 100
